TPU v7x, 32 devices: a whole 2x2x4 slice. The times are simulated.
32 devices in a mesh: expert: 16 (over z, y, x), hidden: 2 (over core).
Axes of the slice: x: 2, y: 2, z: 4, core: 2. Of those that a mesh axis runs over, the one named last changes fastest.
Arguments:
- tokens: bfloat16 [1024, 4096], P('expert', 'hidden'), may hold values from -6 to 6
- expert_ids: int32 [1024, 8], P('expert'), may hold values from 0 to 15, all different within a row; in each aligned block of 64 rows (0 to 63, 64 to 127, ...) at most 64 rows name the same one
- gate_weights: float32 [1024, 8], P('expert'), may hold values from 0.05 to 0.5
- gate_proj: bfloat16 [16, 1536, 4096], P('expert', 'hidden'), may hold values from -0.09375 to 0.09375
- up_proj: bfloat16 [16, 1536, 4096], P('expert', 'hidden'), may hold values from -0.09375 to 0.09375
- down_proj: bfloat16 [16, 1536, 4096], P('expert', None, 'hidden'), may hold values from -0.15625 to 0.15625
Outputs:
- moe_out: bfloat16 [1024, 4096], P('expert', 'hidden')
Inputs may be any that keep to these rules, and one draw needn't show every extreme that they name: `expert_ids`: each row names 8 different experts; in each aligned block of 64 rows no expert is named by more than 64 rows.
All inputs are finite; a program needn't handle non-finite values.
Results may differ from a plain program's by a relative error of at most 0.0057.
Values may be sent and summed in bfloat16 or wider, within the bound.
A program may use at most 64 MiB of HBM per device.

v0:
```python
import functools

import jax
import jax.numpy as jnp
from jax import lax
from jax.experimental import pallas as pl
from jax.experimental.pallas import tpu as pltpu
from jax.sharding import PartitionSpec as P

MESH = pl.DeviceIdType.MESH
NZ, NY, NX = 4, 2, 2
ROWS = 16
TILE = 256
THIRD = 256


def routed(tokens, expert_ids, gate_weights, gate_proj, up_proj, down_proj):
    local_count = gate_proj.shape[0]
    experts_all = local_count * lax.axis_size("expert")
    tok_rows = tokens.shape[0]
    top_count = expert_ids.shape[1]
    capacity = 2 * tok_rows * top_count // experts_all
    flat_ids = expert_ids.reshape(-1)
    onehot = (flat_ids[:, None] == jnp.arange(experts_all, dtype=jnp.int32)[None, :]).astype(
        jnp.int32
    )
    slot_index = jnp.sum((jnp.cumsum(onehot, axis=0) - onehot) * onehot, axis=1)
    position = flat_ids * capacity + slot_index
    token_of = jnp.arange(tok_rows * top_count, dtype=jnp.int32) // top_count
    full_rows = lax.all_gather(tokens, "hidden", axis=1, tiled=True)
    packed = jnp.zeros((experts_all * capacity, full_rows.shape[1]), full_rows.dtype)
    packed = packed.at[position].set(full_rows[token_of])
    arrived = lax.all_to_all(
        packed.reshape(experts_all, capacity, full_rows.shape[1]),
        "expert",
        split_axis=0,
        concat_axis=1,
        tiled=True,
    )
    gate_sum = jnp.einsum("lrd,lfd->lfr", arrived, gate_proj, preferred_element_type=jnp.float32)
    up_sum = jnp.einsum("lrd,lfd->lfr", arrived, up_proj, preferred_element_type=jnp.float32)
    activation = (jax.nn.silu(gate_sum) * up_sum).astype(jnp.bfloat16)
    expert_out = jnp.einsum(
        "lfr,lfd->lrd",
        lax.all_gather(activation, "hidden", axis=1, tiled=True),
        down_proj,
        preferred_element_type=jnp.float32,
    ).astype(jnp.bfloat16)
    returned = lax.all_to_all(expert_out, "expert", split_axis=1, concat_axis=0, tiled=True)
    gathered = returned.reshape(experts_all * capacity, returned.shape[2])[position]
    gathered = gathered.reshape(tok_rows, top_count, returned.shape[2]).astype(jnp.float32)
    mixed = jnp.sum(gathered * gate_weights[:, :, None], axis=1)
    return mixed.astype(jnp.bfloat16)


def dense_kernel(
    tok_ref, wmat_ref, gate_hbm, up_hbm, down_hbm, out_ref,
    x_buf, xa_buf, w_buf, w_col, gate, up, down, act,
    part, parta, red1, red2, red3, reda1, reda2, reda3,
    local_sem, send_sem, recv_sem,
):
    chunks = tok_ref.shape[0] // ROWS
    wide = x_buf.shape[-1]
    half = tok_ref.shape[1]
    rows = NZ * NY * NX * ROWS
    hid = gate.shape[0]
    f32, bf16 = jnp.float32, jnp.bfloat16
    me = lax.axis_index("expert")
    core = lax.axis_index("hidden")
    z, y, x = me // (NY * NX), (me // NX) % NY, me % NX

    def at(zz, yy, xx):
        return ((zz * NY + yy) * NX + xx, core)

    x_peer, y_peer, sibling = at(z, y, 1 - x), at(z, 1 - y, x), (me, 1 - core)
    z_of = [lax.rem(z + d, NZ) for d in range(NZ)]
    z_peers = [at(z_of[d], y, x) for d in range(NZ)]

    loads = [
        pltpu.make_async_copy(src, dst, local_sem.at[i])
        for i, (src, dst) in enumerate(((gate_hbm, gate), (up_hbm, up), (down_hbm, down)))
    ]
    for load in loads:
        load.start()

    barrier = pltpu.get_barrier_semaphore()
    peers = [x_peer, y_peer, sibling] + z_peers[1:]
    for peer in peers:
        pl.semaphore_signal(barrier, inc=1, device_id=peer, device_id_type=MESH)
    for c in range(chunks):
        for p in range(2):
            x_buf[(c * 2 + core) * 2 + p, z, y, x] = tok_ref[
                c * ROWS : (c + 1) * ROWS, p * wide : (p + 1) * wide
            ]
        xa_buf[c * 2 + core, z, y, x] = tok_ref[c * ROWS : (c + 1) * ROWS, 2 * wide :]
    blank = jnp.zeros((wmat_ref.shape[0], 128 - wmat_ref.shape[1]), f32)
    w_buf[z, y, x] = jnp.concatenate([wmat_ref[...], blank], axis=1)
    pl.semaphore_wait(barrier, len(peers))

    sent = []

    def send(src, dst, peer):
        k = len(sent)
        copy = pltpu.make_async_remote_copy(
            src_ref=src, dst_ref=dst, send_sem=send_sem.at[k], recv_sem=recv_sem.at[k],
            device_id=peer, device_id_type=MESH,
        )
        copy.start()
        sent.append(copy)
        return copy

    def arrive(copies):
        for copy in copies:
            copy.wait_recv()

    def move(ref, peer):
        return send(ref, ref, peer)

    def spread_z(c):
        own = x_buf.at[pl.ds((c * 2 + core) * 2, 2), z, y, x]
        return [move(own, z_peers[d]) for d in range(1, NZ)] + [
            move(xa_buf.at[c * 2 + core, z, y, x], x_peer)
        ]

    def spread_1(c):
        i = (c * 2 + core) * 2
        return [
            move(x_buf.at[i, :, y, x], x_peer),
            move(x_buf.at[i + 1, :, y, x], y_peer),
            move(xa_buf.at[c * 2 + core, z, y], y_peer),
        ]

    def spread_2(c):
        i = (c * 2 + core) * 2
        third = xa_buf.at[c * 2 + core, z]
        return [
            move(x_buf.at[i, :, y], y_peer),
            move(x_buf.at[i + 1, :, :, x], x_peer),
        ] + [move(third, z_peers[d]) for d in range(1, NZ)]

    def spread_core(c):
        return [
            move(x_buf.at[pl.ds((c * 2 + core) * 2, 2)], sibling),
            move(xa_buf.at[c * 2 + core], sibling),
        ]

    def gate_up(c):
        def step(n, carry):
            cols = pl.ds(pl.multiple_of(n * TILE, TILE), TILE)
            sums = []
            for weight in (gate, up):
                total = None
                for k in range(6):
                    hh, p = k // 3, k % 3
                    if p < 2:
                        piece = x_buf[c * 4 + hh * 2 + p].reshape(rows, wide)
                    else:
                        piece = xa_buf[c * 2 + hh].reshape(rows, THIRD)
                    low = hh * half + p * wide
                    term = lax.dot_general(
                        piece,
                        weight[cols, low : low + piece.shape[1]],
                        (((1,), (1,)), ((), ())),
                        preferred_element_type=f32,
                    )
                    total = term if total is None else total + term
                sums.append(total)
            g, u = sums
            act[c * 2 + core, :, cols] = ((g / (1.0 + jnp.exp(-g))) * u).astype(bf16)
            return carry

        lax.fori_loop(0, hid // TILE, step, 0)
        return [move(act.at[c * 2 + core], sibling)]

    def down_tile(c, start, size):
        total = None
        for k in range(2):
            term = jnp.dot(
                act[c * 2 + k], down[k * hid : (k + 1) * hid, pl.ds(start, size)],
                preferred_element_type=f32,
            )
            total = term if total is None else total + term
        scale = w_col[c]
        total = total * jnp.concatenate([scale] * (size // 128), axis=1)
        return total.astype(bf16).reshape(NZ, NY, NX, ROWS, size)

    def down_part(c, p):
        def step(n, carry):
            into = pl.ds(pl.multiple_of(n * TILE, TILE), TILE)
            start = pl.multiple_of(p * wide + n * TILE, 128)
            part[c * 2 + p, :, :, :, :, into] = down_tile(c, start, TILE)
            return carry

        lax.fori_loop(0, wide // TILE, step, 0)
        rest = wide % TILE
        if rest:
            part[c * 2 + p, :, :, :, :, wide - rest :] = down_tile(c, (p + 1) * wide - rest, rest)

    def down_all(c):
        down_part(c, 0)
        first = send(part.at[c * 2, :, 1 - y], red1.at[c * 2], y_peer)
        down_part(c, 1)
        second = send(part.at[c * 2 + 1, :, :, 1 - x], red1.at[c * 2 + 1], x_peer)
        parta[c] = down_tile(c, 2 * wide, THIRD)
        return [first, second] + [
            send(parta.at[c, z_of[d]], reda1.at[c, d - 1], z_peers[d]) for d in range(1, NZ)
        ]

    def reduce_1(c, copies):
        copies[0].wait_recv()
        for zz in range(NZ):
            red1[c * 2, zz] = (
                red1[c * 2, zz].astype(f32) + part[c * 2, zz, y].astype(f32)
            ).astype(bf16)
        first = send(red1.at[c * 2, :, 1 - x], red2.at[c * 2], x_peer)
        copies[1].wait_recv()
        for zz in range(NZ):
            for yy in range(NY):
                red1[c * 2 + 1, zz, yy] = (
                    red1[c * 2 + 1, zz, yy].astype(f32) + part[c * 2 + 1, zz, yy, x].astype(f32)
                ).astype(bf16)
        second = send(red1.at[c * 2 + 1, :, 1 - y], red2.at[c * 2 + 1], y_peer)
        arrive(copies[2:])
        total = parta[c, z].astype(f32)
        for d in range(NZ - 1):
            total = total + reda1[c, d].astype(f32)
        parta[c, z] = total.astype(bf16)
        return [first, second, send(parta.at[c, z, 1 - y], reda2.at[c], y_peer)]

    def reduce_2(c, copies):
        for p, (copy, mine) in enumerate(zip(copies, (x, y))):
            copy.wait_recv()
            for zz in range(NZ):
                red2[c * 2 + p, zz] = (
                    red2[c * 2 + p, zz].astype(f32) + red1[c * 2 + p, zz, mine].astype(f32)
                ).astype(bf16)
        out = [
            send(red2.at[pl.ds(c * 2, 2), z_of[d]], red3.at[c, d - 1], z_peers[d])
            for d in range(1, NZ)
        ]
        copies[2].wait_recv()
        reda2[c] = (reda2[c].astype(f32) + parta[c, z, y].astype(f32)).astype(bf16)
        return out + [send(reda2.at[c, 1 - x], reda3.at[c], x_peer)]

    def finish(c, copies):
        arrive(copies)
        for p in range(2):
            total = red2[c * 2 + p, z].astype(f32)
            for d in range(NZ - 1):
                total = total + red3[c, d, p].astype(f32)
            out_ref[c * ROWS : (c + 1) * ROWS, p * wide : (p + 1) * wide] = total.astype(bf16)
        total = reda2[c, x].astype(f32) + reda3[c].astype(f32)
        out_ref[c * ROWS : (c + 1) * ROWS, 2 * wide :] = total.astype(bf16)

    def columns_of_weights():
        lane = lax.broadcasted_iota(jnp.int32, w_buf.shape[3:], 0)
        picked = [
            jnp.sum(jnp.where(lane == me, w_buf[zz, yy, xx], 0.0), axis=0, keepdims=True)
            for zz in range(NZ) for yy in range(NY) for xx in range(NX)
        ]
        square = jnp.concatenate(picked + [jnp.zeros((128 - len(picked), 128), f32)], axis=0)
        turned = square.T
        for c in range(chunks):
            for b in range(len(picked)):
                w_col[c, b * ROWS : (b + 1) * ROWS, :] = jnp.broadcast_to(
                    turned[c * ROWS : (c + 1) * ROWS, b : b + 1], (ROWS, 128)
                )

    za = [None] * chunks
    s1, s2, sc = [None] * chunks, [None] * chunks, [None] * chunks
    aa, r1, r2, r3 = [None] * chunks, [None] * chunks, [None] * chunks, [None] * chunks

    za[0] = spread_z(0)
    wz = [move(w_buf.at[z, y, x], z_peers[d]) for d in range(1, NZ)]
    za[1] = spread_z(1)
    arrive(za[0])
    s1[0] = spread_1(0)
    arrive(wz)
    wx = [move(w_buf.at[:, y, x], x_peer)]
    za[2] = spread_z(2)
    arrive(s1[0])
    s2[0] = spread_2(0)
    arrive(wx)
    wy = [move(w_buf.at[:, y], y_peer)]
    arrive(za[1])
    s1[1] = spread_1(1)
    za[3] = spread_z(3)
    arrive(s1[1])
    s2[1] = spread_2(1)
    arrive(wy)
    columns_of_weights()
    arrive(s2[0])
    sc[0] = spread_core(0)
    arrive(za[2])
    s1[2] = spread_1(2)
    loads[0].wait()
    loads[1].wait()
    loads[2].wait()
    arrive(sc[0])
    aa[0] = gate_up(0)
    arrive(s1[2])
    s2[2] = spread_2(2)
    arrive(s2[1])
    sc[1] = spread_core(1)
    arrive(za[3])
    s1[3] = spread_1(3)
    arrive(sc[1])
    aa[1] = gate_up(1)
    arrive(s1[3])
    s2[3] = spread_2(3)
    arrive(aa[0])
    r1[0] = down_all(0)
    arrive(s2[2])
    sc[2] = spread_core(2)
    arrive(aa[1])
    r1[1] = down_all(1)
    arrive(sc[2])
    aa[2] = gate_up(2)
    r2[0] = reduce_1(0, r1[0])
    arrive(s2[3])
    sc[3] = spread_core(3)
    arrive(aa[2])
    r1[2] = down_all(2)
    arrive(sc[3])
    aa[3] = gate_up(3)
    r2[1] = reduce_1(1, r1[1])
    r3[0] = reduce_2(0, r2[0])
    arrive(aa[3])
    r1[3] = down_all(3)
    r2[2] = reduce_1(2, r1[2])
    r3[1] = reduce_2(1, r2[1])
    finish(0, r3[0])
    r2[3] = reduce_1(3, r1[3])
    r3[2] = reduce_2(2, r2[2])
    finish(1, r3[1])
    r3[3] = reduce_2(3, r2[3])
    finish(2, r3[2])
    finish(3, r3[3])
    for copy in sent:
        copy.wait_send()


def dense(tokens, expert_ids, gate_weights, gate_proj, up_proj, down_proj):
    tok_rows, half = tokens.shape
    experts_all = lax.axis_size("expert")
    hid, width = gate_proj.shape[1:]
    chunks = tok_rows // ROWS
    wide = (half - THIRD) // 2
    rows = experts_all * ROWS
    chosen = expert_ids[None, :, :] == jnp.arange(experts_all, dtype=jnp.int32)[:, None, None]
    wmat = jnp.sum(jnp.where(chosen, gate_weights[None], 0.0), axis=2)
    bf16, f32 = jnp.bfloat16, jnp.float32
    vmem = pl.BlockSpec(memory_space=pltpu.VMEM)
    hbm = pl.BlockSpec(memory_space=pl.ANY)
    copies = chunks * 27 + 5
    return pl.pallas_call(
        dense_kernel,
        out_shape=jax.ShapeDtypeStruct((tok_rows, half), bf16),
        in_specs=[vmem, vmem, hbm, hbm, hbm],
        out_specs=vmem,
        scratch_shapes=[
            pltpu.VMEM((chunks * 4, NZ, NY, NX, ROWS, wide), bf16),
            pltpu.VMEM((chunks * 2, NZ, NY, NX, ROWS, THIRD), bf16),
            pltpu.VMEM((NZ, NY, NX, experts_all, 128), f32),
            pltpu.VMEM((chunks, rows, 128), f32),
            pltpu.VMEM((hid, width), bf16),
            pltpu.VMEM((hid, width), bf16),
            pltpu.VMEM((2 * hid, half), bf16),
            pltpu.VMEM((chunks * 2, rows, hid), bf16),
            pltpu.VMEM((chunks * 2, NZ, NY, NX, ROWS, wide), bf16),
            pltpu.VMEM((chunks, NZ, NY, NX, ROWS, THIRD), bf16),
            pltpu.VMEM((chunks * 2, NZ, 2, ROWS, wide), bf16),
            pltpu.VMEM((chunks * 2, NZ, ROWS, wide), bf16),
            pltpu.VMEM((chunks, NZ - 1, 2, ROWS, wide), bf16),
            pltpu.VMEM((chunks, NZ - 1, NY, NX, ROWS, THIRD), bf16),
            pltpu.VMEM((chunks, NX, ROWS, THIRD), bf16),
            pltpu.VMEM((chunks, ROWS, THIRD), bf16),
            pltpu.SemaphoreType.DMA((3,)),
            pltpu.SemaphoreType.DMA((copies,)),
            pltpu.SemaphoreType.DMA((copies,)),
        ],
        compiler_params=pltpu.CompilerParams(
            collective_id=0, has_side_effects=True, vmem_limit_bytes=60 * 1024 * 1024
        ),
    )(tokens, wmat, gate_proj[0], up_proj[0], down_proj[0])


def solution(mesh):
    in_specs = (
        P("expert", "hidden"),
        P("expert", None),
        P("expert", None),
        P("expert", "hidden", None),
        P("expert", "hidden", None),
        P("expert", None, "hidden"),
    )
    out_specs = P("expert", "hidden")
    whole_blocks = mesh.shape["expert"] == NZ * NY * NX and mesh.shape["hidden"] == 2
    return jax.shard_map(
        dense if whole_blocks else routed,
        mesh=mesh, in_specs=in_specs, out_specs=out_specs, check_vma=False,
    )
```

profile of v0, /device:TPU:0, one launch (start us, length us, event | category | flops | bytes accessed | tf_op | source)
XLA Modules:
  0.0 97.1 jit_solution(17723656011442270170)
XLA Ops:
  0.0 1.3 %select_reduce_fusion.wmat_ref = f32[16,64]{1,0:T(8,128)} fusion(f32[64,8]{0,1:T(8,128)} %param.8, s32[64,8]{0,1:T(8,128)} %param.7), kind=kLoop, calls=%fused_computation | loop fusion | flops 23552 | bytes 8192 | tf_op jit(solution)/shard_map/reduce_sum | solution.py:351
  1.3 94.0 %shard_map.64 = bf16[64,2048]{1,0:T(8,128)(2,1)} custom-call(bf16[64,2048]{1,0:T(8,128)(2,1)} %tok_ref.1, f32[16,64]{1,0:T(8,128)} %select_reduce_fusion.wmat_ref, bf16[768,4096]{1,0:T(8,128)(2,1)} %bitcast.3, bf16[768,4096]{1,0:T(8,128)(2,1)} %bitcast.4, bf16[1536,2048]{1,0:T(8,128)(2,1)} %bitcast.5), custom_call_target="tpu_custom_call" | custom-call | tf_op jit(solution)/shard_map/pallas_call | solution.py:356
  95.4 1.7 %copy.10 = bf16[64,2048]{1,0:T(8,128)(2,1)} copy(bf16[64,2048]{1,0:T(8,128)(2,1)} %shard_map.64) | data formatting | bytes 524288
where the time goes:
time: 97.3 us; the launch traced here: 97.1 us
  Pallas kernels  94 us (97%)
  local copies, waits for them, and re-layouts  1.67 us (2%)
  other arithmetic  1.32 us (1%)
    pallas_call x1, Pallas kernels, dense(): pl.pallas_call(dense_kernel, out_shape=jax.ShapeDtypeStruct((tok_rows, ha...  94 us

commit v1 on v0

--- a/solution.py
+++ b/solution.py
@@ -145,31 +145,26 @@
         ]
 
     def gate_up(c):
-        def step(n, carry):
-            cols = pl.ds(pl.multiple_of(n * TILE, TILE), TILE)
-            sums = []
-            for weight in (gate, up):
-                total = None
-                for k in range(6):
-                    hh, p = k // 3, k % 3
-                    if p < 2:
-                        piece = x_buf[c * 4 + hh * 2 + p].reshape(rows, wide)
-                    else:
-                        piece = xa_buf[c * 2 + hh].reshape(rows, THIRD)
-                    low = hh * half + p * wide
-                    term = lax.dot_general(
-                        piece,
-                        weight[cols, low : low + piece.shape[1]],
-                        (((1,), (1,)), ((), ())),
-                        preferred_element_type=f32,
-                    )
-                    total = term if total is None else total + term
-                sums.append(total)
-            g, u = sums
-            act[c * 2 + core, :, cols] = ((g / (1.0 + jnp.exp(-g))) * u).astype(bf16)
-            return carry
-
-        lax.fori_loop(0, hid // TILE, step, 0)
+        sums = []
+        for weight in (gate, up):
+            total = None
+            for k in range(6):
+                hh, p = k // 3, k % 3
+                if p < 2:
+                    piece = x_buf[c * 4 + hh * 2 + p].reshape(rows, wide)
+                else:
+                    piece = xa_buf[c * 2 + hh].reshape(rows, THIRD)
+                low = hh * half + p * wide
+                term = lax.dot_general(
+                    weight[:, low : low + piece.shape[1]],
+                    piece,
+                    (((1,), (1,)), ((), ())),
+                    preferred_element_type=f32,
+                )
+                total = term if total is None else total + term
+            sums.append(total)
+        g, u = sums
+        act[c * 2 + core] = ((g / (1.0 + jnp.exp(-g))) * u).T.astype(bf16)
         return [move(act.at[c * 2 + core], sibling)]
 
     def down_tile(c, start, size):

time: 97.3 us -> 97.6 us (level)
  no operation moved by 1% of the time
where the time goes in v1:
time: 97.6 us; the launch traced here: 97.4 us
  Pallas kernels  94.4 us (97%)
  local copies, waits for them, and re-layouts  1.67 us (2%)
  other arithmetic  1.32 us (1%)
    pallas_call x1, Pallas kernels, dense(): pl.pallas_call(dense_kernel, out_shape=jax.ShapeDtypeStruct((tok_rows, ha...  94.4 us

profile of v1, /device:TPU:0, one launch (start us, length us, event | category | flops | bytes accessed | tf_op | source)
XLA Modules:
  0.0 97.4 jit_solution(14461428397218978755)
XLA Ops:
  0.0 1.3 %select_reduce_fusion.wmat_ref = f32[16,64]{1,0:T(8,128)} fusion(f32[64,8]{0,1:T(8,128)} %param.8, s32[64,8]{0,1:T(8,128)} %param.7), kind=kLoop, calls=%fused_computation | loop fusion | flops 23552 | bytes 8192 | tf_op jit(solution)/shard_map/reduce_sum | solution.py:346
  1.3 94.4 %shard_map.64 = bf16[64,2048]{1,0:T(8,128)(2,1)} custom-call(bf16[64,2048]{1,0:T(8,128)(2,1)} %tok_ref.1, f32[16,64]{1,0:T(8,128)} %select_reduce_fusion.wmat_ref, bf16[768,4096]{1,0:T(8,128)(2,1)} %bitcast.3, bf16[768,4096]{1,0:T(8,128)(2,1)} %bitcast.4, bf16[1536,2048]{1,0:T(8,128)(2,1)} %bitcast.5), custom_call_target="tpu_custom_call" | custom-call | tf_op jit(solution)/shard_map/pallas_call | solution.py:351
  95.7 1.7 %copy.10 = bf16[64,2048]{1,0:T(8,128)(2,1)} copy(bf16[64,2048]{1,0:T(8,128)(2,1)} %shard_map.64) | data formatting | bytes 524288

commit v2 on v0

--- a/solution.py
+++ b/solution.py
@@ -198,11 +198,14 @@
 
     def down_all(c):
         down_part(c, 0)
-        first = send(part.at[c * 2, :, 1 - y], red1.at[c * 2], y_peer)
         down_part(c, 1)
-        second = send(part.at[c * 2 + 1, :, :, 1 - x], red1.at[c * 2 + 1], x_peer)
         parta[c] = down_tile(c, 2 * wide, THIRD)
-        return [first, second] + [
+
+    def reduce_0(c):
+        return [
+            send(part.at[c * 2, :, 1 - y], red1.at[c * 2], y_peer),
+            send(part.at[c * 2 + 1, :, :, 1 - x], red1.at[c * 2 + 1], x_peer),
+        ] + [
             send(parta.at[c, z_of[d]], reda1.at[c, d - 1], z_peers[d]) for d in range(1, NZ)
         ]
 
@@ -309,24 +312,28 @@
     arrive(s1[3])
     s2[3] = spread_2(3)
     arrive(aa[0])
-    r1[0] = down_all(0)
+    down_all(0)
+    r1[0] = reduce_0(0)
     arrive(s2[2])
     sc[2] = spread_core(2)
     arrive(aa[1])
-    r1[1] = down_all(1)
+    down_all(1)
     arrive(sc[2])
     aa[2] = gate_up(2)
-    r2[0] = reduce_1(0, r1[0])
     arrive(s2[3])
     sc[3] = spread_core(3)
+    r1[1] = reduce_0(1)
     arrive(aa[2])
-    r1[2] = down_all(2)
+    down_all(2)
+    r1[2] = reduce_0(2)
+    r2[0] = reduce_1(0, r1[0])
     arrive(sc[3])
     aa[3] = gate_up(3)
     r2[1] = reduce_1(1, r1[1])
     r3[0] = reduce_2(0, r2[0])
     arrive(aa[3])
-    r1[3] = down_all(3)
+    down_all(3)
+    r1[3] = reduce_0(3)
     r2[2] = reduce_1(2, r1[2])
     r3[1] = reduce_2(1, r2[1])
     finish(0, r3[0])

time: 97.3 us -> 102 us (1.048)
  Pallas kernels: 94 us -> 98.3 us
    pallas_call x1, Pallas kernels: 94 us -> 98.3 us  [dense(): pl.pallas_call(dense_kernel, out_shape=jax.ShapeDtypeStruct((tok_rows, ha...]
where the time goes in v2:
time: 102 us; the launch traced here: 101 us
  Pallas kernels  98.3 us (96%)
  local copies, waits for them, and re-layouts  1.67 us (2%)
  other arithmetic  1.32 us (1%)
    pallas_call x1, Pallas kernels, dense(): pl.pallas_call(dense_kernel, out_shape=jax.ShapeDtypeStruct((tok_rows, ha...  98.3 us

profile of v2, /device:TPU:0, one launch (start us, length us, event | category | flops | bytes accessed | tf_op | source)
XLA Modules:
  0.0 101.3 jit_solution(12256717435450900904)
XLA Ops:
  0.0 1.3 %select_reduce_fusion.wmat_ref = f32[16,64]{1,0:T(8,128)} fusion(f32[64,8]{0,1:T(8,128)} %param.8, s32[64,8]{0,1:T(8,128)} %param.7), kind=kLoop, calls=%fused_computation | loop fusion | flops 23552 | bytes 8192 | tf_op jit(solution)/shard_map/reduce_sum | solution.py:358
  1.3 98.3 %shard_map.64 = bf16[64,2048]{1,0:T(8,128)(2,1)} custom-call(bf16[64,2048]{1,0:T(8,128)(2,1)} %tok_ref.1, f32[16,64]{1,0:T(8,128)} %select_reduce_fusion.wmat_ref, bf16[768,4096]{1,0:T(8,128)(2,1)} %bitcast.3, bf16[768,4096]{1,0:T(8,128)(2,1)} %bitcast.4, bf16[1536,2048]{1,0:T(8,128)(2,1)} %bitcast.5), custom_call_target="tpu_custom_call" | custom-call | tf_op jit(solution)/shard_map/pallas_call | solution.py:363
  99.7 1.7 %copy.10 = bf16[64,2048]{1,0:T(8,128)(2,1)} copy(bf16[64,2048]{1,0:T(8,128)(2,1)} %shard_map.64) | data formatting | bytes 524288
